TPU v7x, 32 devices: a whole 2x2x4 slice. The times are simulated.
32 devices in a mesh: kxy: 8 (over y, x, core), kz: 4 (over z).
Axes of the slice: x: 2, y: 2, z: 4, core: 2. Of those that a mesh axis runs over, the one named last changes fastest.
Arguments:
- factors: float32 [8, 4, 2, 384, 1024], P('kxy', 'kz'), may hold values from -0.9 to 0.9
- occ_energy: float32 [8, 4, 8], P('kxy', 'kz'), may hold values from -2 to -0.5
- vir_energy: float32 [8, 4, 128], P('kxy', 'kz'), may hold values from 0.5 to 3
- shifts: int32 [2, 2], replicated, may hold values from 0 to 3, as said below
Outputs:
- gradient: float32 [8, 4, 2, 384, 1024], P('kxy', 'kz')
Inputs may be any that keep to these rules, and one draw needn't show every extreme that they name: `shifts`: row 0 (the momentum transfer) has both entries between 1 and 3. Row 1 is the partner displacement; it is always (3, 3).
All inputs are finite; a program needn't handle non-finite values.
Results may differ from a plain program's by a relative error of at most 0.0001.
Values sent between devices are 32-bit elements; how exact they have to be, the bound alone decides.
A program may use at most 64 MiB of HBM per device.

v0:
```python
import jax
import jax.numpy as jnp
from jax import lax
from jax.sharding import PartitionSpec as P

REACH = 4


def shifted(x, axis, by):
    size = lax.axis_size(axis)
    return lax.ppermute(x, axis, [(i, (i + by) % size) for i in range(size)])


def product(left, right):
    return jnp.dot(left, right, precision=lax.Precision.HIGHEST, preferred_element_type=jnp.float32)


def inner_first(left, right):
    return lax.dot_general(
        left,
        right,
        (((0,), (0,)), ((), ())),
        precision=lax.Precision.HIGHEST,
        preferred_element_type=jnp.float32,
    )


def inner_last(left, right):
    return lax.dot_general(
        left,
        right,
        (((1,), (1,)), ((), ())),
        precision=lax.Precision.HIGHEST,
        preferred_element_type=jnp.float32,
    )


def select(chosen, arrived, kept):
    return jax.tree.map(lambda fresh, stale: jnp.where(chosen, fresh, stale), arrived, kept)


def pull_partner(payload, step_x, step_z):
    sections = (REACH - 1).bit_length()
    for level in range(sections):
        arrived = shifted(payload, "kxy", -(1 << level))
        payload = select(step_x >> level & 1 == 1, arrived, payload)
    for level in range(sections):
        arrived = shifted(payload, "kz", -(1 << level))
        payload = select(step_z >> level & 1 == 1, arrived, payload)
    return payload


def pull_behind(payload, step_x, step_z):
    sections = (REACH - 1).bit_length()
    for level in range(sections):
        arrived = shifted(payload, "kxy", 1 << level)
        payload = select(step_x >> level & 1 == 1, arrived, payload)
    for level in range(sections):
        arrived = shifted(payload, "kz", 1 << level)
        payload = select(step_z >> level & 1 == 1, arrived, payload)
    return payload


def amplitudes(first, second, occ_first, vir_first, occ_second, vir_second):
    real_v = inner_first(first[0], second[0]) + inner_first(first[1], second[1])
    imag_v = inner_first(first[1], second[0]) - inner_first(first[0], second[1])
    gap_first = (vir_first[None, :] - occ_first[:, None]).reshape(-1)
    gap_second = (vir_second[None, :] - occ_second[:, None]).reshape(-1)
    denominator = gap_first[:, None] + gap_second[None, :]
    return (real_v / denominator, imag_v / denominator)


def own_term(partner, real_t, imag_t):
    real_g = inner_last(partner[0], real_t) - inner_last(partner[1], imag_t)
    imag_g = inner_last(partner[0], imag_t) + inner_last(partner[1], real_t)
    return jnp.stack([real_g, imag_g])


def partner_term(first, real_t, imag_t):
    real_h = product(first[0], real_t) + product(first[1], imag_t)
    imag_h = product(first[1], real_t) - product(first[0], imag_t)
    return jnp.stack([real_h, imag_h])


def body(factors, occ_energy, vir_energy, shifts):
    own_panel = factors[0, 0]
    occ_self = occ_energy[0, 0]
    vir_moved = vir_energy[0, 0]
    sections = (REACH - 1).bit_length()
    for level in range(sections):
        arrived = shifted(vir_moved, "kxy", -(1 << level))
        vir_moved = jnp.where(shifts[0, 0] >> level & 1 == 1, arrived, vir_moved)
    for level in range(sections):
        arrived = shifted(vir_moved, "kz", -(1 << level))
        vir_moved = jnp.where(shifts[0, 1] >> level & 1 == 1, arrived, vir_moved)
    step_x = shifts[1, 0]
    step_z = shifts[1, 1]
    partner, occ_part, vir_part = pull_partner((own_panel, occ_self, vir_moved), step_x, step_z)
    real_t, imag_t = amplitudes(own_panel, partner, occ_self, vir_moved, occ_part, vir_part)
    gradient_sum = own_term(partner, real_t, imag_t)
    behind, occ_behind, vir_behind = pull_behind((own_panel, occ_self, vir_moved), step_x, step_z)
    back_real, back_imag = amplitudes(
        behind, own_panel, occ_behind, vir_behind, occ_self, vir_moved
    )
    gradient_sum = gradient_sum + partner_term(behind, back_real, back_imag)
    return (-gradient_sum)[None, None]


def solution(mesh):
    placed = (P("kxy", "kz", None, None, None), P("kxy", "kz", None), P("kxy", "kz", None), P())
    return jax.shard_map(
        body,
        mesh=mesh,
        in_specs=placed,
        out_specs=P("kxy", "kz", None, None, None),
        check_vma=False,
    )
```

profile of v0, /device:TPU:0, one launch (start us, length us, event | category | flops | bytes accessed | tf_op | source)
XLA Modules:
  0.0 646.2 jit_solution(13464080773486967740)
XLA Ops:
  0.0 3.3 collective-permute-start
  3.3 1.5 fusion.25
  5.4 65.8 %collective-permute-done = f32[2,384,1024]{2,1,0:T(8,128)S(1)} collective-permute-done((f32[2,384,1024]{2,1,0:T(8,128)}, f32[2,384,1024]{2,1,0:T(8,128)S(1)}, u32[]{:S(2)}, u32[]{:S(2)}) %collective-permute-start) | collective-permute-done | bytes 3145760 | tf_op jit(solution)/shard_map/ppermute | solution.py:11
  71.2 1.9 collective-permute-done.16
  73.1 3.3 broadcast_select_fusion
  76.4 2.9 collective-permute-start.1
  79.9 68.4 %collective-permute-done.17 = f32[2,384,1024]{2,1,0:T(8,128)S(1)} collective-permute-done((f32[2,384,1024]{2,1,0:T(8,128)S(1)}, f32[2,384,1024]{2,1,0:T(8,128)S(1)}, u32[]{:S(2)}, u32[]{:S(2)}) %collective-permute-start.17) | collective-permute-done | bytes 3145760 | tf_op jit(solution)/shard_map/ppermute | solution.py:11
  148.4 0.7 broadcast_select_fusion.2
  149.0 1.6 collective-permute-start.18
  150.7 0.5 collective-permute-start.24
  151.2 2.1 collective-permute-start.4
  157.3 54.9 %collective-permute-done.12 = f32[8]{0:T(128)S(1)} collective-permute-done((f32[8]{0:T(128)S(1)}, f32[8]{0:T(128)S(1)}, u32[]{:S(2)}, u32[]{:S(2)}) %collective-permute-start.12) | collective-permute-done | bytes 64 | tf_op jit(solution)/shard_map/ppermute | solution.py:11
  212.2 2.6 collective-permute-start.25
  214.8 0.3 collective-permute-start.13
  215.1 1.5 collective-permute-done.25
  216.6 1.6 collective-permute-start.26
  218.2 0.1 collective-permute-done.13
  218.4 3.6 collective-permute-start.14
  222.0 0.8 collective-permute-start.27
  222.8 0.8 collective-permute-start.5
  223.6 2.5 collective-permute-start.15
  226.1 0.2 collective-permute-done.5
  226.3 1.3 collective-permute-start.6
  227.7 0.7 broadcast_select_fusion.3
  228.3 2.3 collective-permute-start.2
  230.7 1.4 collective-permute-start.7
  232.1 1.0 broadcast_select_fusion.4
  233.0 1.7 collective-permute-start.19
  234.7 132.3 %collective-permute-done.7 = f32[128]{0:T(128)S(1)} collective-permute-done((f32[128]{0:T(128)S(1)}, f32[128]{0:T(128)S(1)}, u32[]{:S(2)}, u32[]{:S(2)}) %collective-permute-start.7) | collective-permute-done | bytes 544 | tf_op jit(solution)/shard_map/ppermute | solution.py:11
  366.9 2.6 collective-permute-start.8
  369.6 1.2 collective-permute-done.20
  370.8 0.1 collective-permute-done.8
  370.9 1.7 collective-permute-start.21
  372.7 1.2 collective-permute-start.9
  373.9 1.4 collective-permute-done.21
  375.3 0.9 collective-permute-done.9
  376.2 3.1 collective-permute-start.10
  379.4 1.3 collective-permute-done.22
  380.7 53.3 %collective-permute-start.23 = (f32[128]{0:T(128)S(1)}, f32[128]{0:T(128)S(1)}, u32[]{:S(2)}, u32[]{:S(2)}) collective-permute-start(f32[128]{0:T(128)S(1)} %broadcast_select_fusion.20), channel_id=1, source_target_pairs={{0,2},{1,3},{2,0},{3,1},{4,6},{5,7},{6,4},{7,5},{8,10},{9,11},{10,... | collective-permute-start | bytes 1544 | tf_op jit(solution)/shard_map/ppermute | solution.py:11
  434.0 0.1 collective-permute-start.11
  434.0 1.4 collective-permute-done.23
  435.6 1.0 broadcast_select_fusion.5
  436.5 3.0 collective-permute-start.3
  439.6 1.0 broadcast_select_fusion.6
  440.6 0.9 copy-done
  441.5 6.7 %fusion.1 = f32[1024,1024]{1,0:T(8,128)S(1)} fusion(f32[2,384,1024]{2,1,0:T(8,128)S(1)} %broadcast_select_fusion.6, f32[1,1,2,384,1024]{4,3,2,1,0:T(8,128)S(1)} %copy-done), kind=kOutput, calls=%fused_computation.10 | convolution fusion | flops 4831838208 | bytes 7340032 | tf_op jit(solution)/shard_map/dot_general | solution.py:19
  448.2 7.2 %fusion.3 = f32[1024,1024]{1,0:T(8,128)S(1)} fusion(f32[2,384,1024]{2,1,0:T(8,128)S(1)} %broadcast_select_fusion.6, f32[1,1,2,384,1024]{4,3,2,1,0:T(8,128)S(1)} %copy-done), kind=kOutput, calls=%fused_computation.12 | convolution fusion | flops 4831838208 | bytes 7340032 | tf_op jit(solution)/shard_map/dot_general | solution.py:19
  455.4 7.4 %add_divide_fusion = f32[1024,1024]{1,0:T(8,128)S(1)} fusion(f32[1024,1024]{1,0:T(8,128)S(1)} %fusion.1, f32[1024]{0:T(1024)S(1)} %subtract_bitcast_fusion.4, f32[1024]{0:T(1024)S(1)} %subtract_bitcast_fusion.2, f32[2,384,1024]{2,1,0:T(8,128)S(1)} %broadcast_select_fusion.6, f32[1,1,2,384,1024]{4,3,2,1,0:T(8,128)S(1)} %copy-done), kind=kOutput, calls=%fused_computation | convolution fusion | flops 4834983936 | bytes 11542528 | tf_op jit(solution)/shard_map/dot_general | solution.py:19
  462.8 5.5 fusion.16
  468.2 5.3 fusion.15
  473.5 100.2 %collective-permute-done.3 = f32[2,384,1024]{2,1,0:T(8,128)S(1)} collective-permute-done((f32[2,384,1024]{2,1,0:T(8,128)S(1)}, f32[2,384,1024]{2,1,0:T(8,128)S(1)}, u32[]{:S(2)}, u32[]{:S(2)}) %collective-permute-start.3) | collective-permute-done | bytes 3145760 | tf_op jit(solution)/shard_map/ppermute | solution.py:11
  573.8 1.0 broadcast_select_fusion.7
  574.7 7.0 %fusion.10 = f32[1024,1024]{1,0:T(8,128)S(1)} fusion(f32[2,384,1024]{2,1,0:T(8,128)S(1)} %broadcast_select_fusion.7, f32[1,1,2,384,1024]{4,3,2,1,0:T(8,128)S(1)} %copy-done), kind=kOutput, calls=%fused_computation.19 | convolution fusion | flops 4831838208 | bytes 7340032 | tf_op jit(solution)/shard_map/dot_general | solution.py:19
  581.7 6.7 %fusion.6 = f32[1024,1024]{1,0:T(8,128)S(1)} fusion(f32[2,384,1024]{2,1,0:T(8,128)S(1)} %broadcast_select_fusion.7, f32[1,1,2,384,1024]{4,3,2,1,0:T(8,128)S(1)} %copy-done), kind=kOutput, calls=%fused_computation.15 | convolution fusion | flops 4831838208 | bytes 7340032 | tf_op jit(solution)/shard_map/dot_general | solution.py:19
  588.5 7.8 %add_divide_fusion.1 = f32[1024,1024]{1,0:T(8,128)S(1)} fusion(f32[1024,1024]{1,0:T(8,128)S(1)} %fusion.3, f32[1024]{0:T(1024)S(1)} %subtract_bitcast_fusion.4, f32[1024]{0:T(1024)S(1)} %subtract_bitcast_fusion.2, f32[2,384,1024]{2,1,0:T(8,128)S(1)} %broadcast_select_fusion.6, f32[1,1,2,384,1024]{4,3,2,1,0:T(8,128)S(1)} %copy-done), kind=kOutput, calls=%fused_computation.1 | convolution fusion | flops 4834983936 | bytes 11542528 | tf_op jit(solution)/shard_map/dot_general | solution.py:19
  596.3 5.3 add_bitcast_fusion
  601.5 5.5 subtract_bitcast_fusion
  607.0 7.4 %add_divide_fusion.2 = f32[1024,1024]{0,1:T(8,128)S(1)} fusion(f32[1024,1024]{1,0:T(8,128)S(1)} %fusion.10, f32[1024]{0:T(1024)S(1)} %subtract_bitcast_fusion.3, f32[1024]{0:T(1024)S(1)} %subtract_bitcast_fusion.4, f32[2,384,1024]{2,1,0:T(8,128)S(1)} %broadcast_select_fusion.7, f32[1,1,2,384,1024]{4,3,2,1,0:T(8,128)S(1)} %copy-done), kind=kOutput, calls=%fused_computation.2 | convolution fusion | flops 4834983936 | bytes 11542528 | tf_op jit(solution)/shard_map/dot_general | solution.py:19
  614.4 5.3 fusion.14
  619.7 7.2 %add_divide_fusion.3 = f32[1024,1024]{0,1:T(8,128)S(1)} fusion(f32[1024,1024]{1,0:T(8,128)S(1)} %fusion.6, f32[1024]{0:T(1024)S(1)} %subtract_bitcast_fusion.3, f32[1024]{0:T(1024)S(1)} %subtract_bitcast_fusion.4, f32[2,384,1024]{2,1,0:T(8,128)S(1)} %broadcast_select_fusion.7, f32[1,1,2,384,1024]{4,3,2,1,0:T(8,128)S(1)} %copy-done), kind=kOutput, calls=%fused_computation.3 | convolution fusion | flops 4834983936 | bytes 11542528 | tf_op jit(solution)/shard_map/dot_general | solution.py:19
  626.9 5.3 fusion.13
  632.2 5.5 subtract_bitcast_fusion.1
  637.7 5.3 add_bitcast_fusion.1
  643.0 2.7 fusion
  (44 shorter events, 0.4 us)
Async XLA Ops:
  0.0 71.2 %collective-permute-start = (f32[2,384,1024]{2,1,0:T(8,128)}, f32[2,384,1024]{2,1,0:T(8,128)S(1)}, u32[]{:S(2)}, u32[]{:S(2)}) collective-permute-start(f32[2,384,1024]{2,1,0:T(8,128)} %bitcast.84), channel_id=1, source_target_pairs={{0,28},{4,0},{8,4},{12,8},{16,12},{20,16},{24,20},{28,24},{1,29},{... | collective-permute-start | bytes 9437192 | tf_op jit(solution)/shard_map/ppermute | solution.py:11
  3.3 69.7 %collective-permute-start.16 = (f32[2,384,1024]{2,1,0:T(8,128)}, f32[2,384,1024]{2,1,0:T(8,128)S(1)}, u32[]{:S(2)}, u32[]{:S(2)}) collective-permute-start(f32[2,384,1024]{2,1,0:T(8,128)} %bitcast.85), channel_id=1, source_target_pairs={{0,4},{4,8},{8,12},{12,16},{16,20},{20,24},{24,28},{28,0},{1,5},{5... | collective-permute-start | bytes 9437192 | tf_op jit(solution)/shard_map/ppermute | solution.py:11
  76.4 72.0 %collective-permute-start.17 = (f32[2,384,1024]{2,1,0:T(8,128)S(1)}, f32[2,384,1024]{2,1,0:T(8,128)S(1)}, u32[]{:S(2)}, u32[]{:S(2)}) collective-permute-start(f32[2,384,1024]{2,1,0:T(8,128)S(1)} %get-tuple-element.5), channel_id=1, source_target_pairs={{0,8},{4,12},{8,16},{12,20},{16,24},{20,28},{24,0},{28,4},{1,9},{5... | collective-permute-start | bytes 9437192 | tf_op jit(solution)/shard_map/ppermute | solution.py:11
  76.4 151.2 %collective-permute-start.1 = (f32[2,384,1024]{2,1,0:T(8,128)S(1)}, f32[2,384,1024]{2,1,0:T(8,128)S(1)}, u32[]{:S(2)}, u32[]{:S(2)}) collective-permute-start(f32[2,384,1024]{2,1,0:T(8,128)S(1)} %get-tuple-element.6), channel_id=1, source_target_pairs={{0,24},{4,28},{8,0},{12,4},{16,8},{20,12},{24,16},{28,20},{1,25},{... | collective-permute-start | bytes 9437192 | tf_op jit(solution)/shard_map/ppermute | solution.py:11
  148.4 2.3 copy-start.1
  148.4 2.8 copy-start.2
  149.0 83.0 %collective-permute-start.18 = (f32[2,384,1024]{2,1,0:T(8,128)S(1)}, f32[2,384,1024]{2,1,0:T(8,128)S(1)}, u32[]{:S(2)}, u32[]{:S(2)}) collective-permute-start(f32[2,384,1024]{2,1,0:T(8,128)S(1)} %broadcast_select_fusion.2), channel_id=1, source_target_pairs={{0,1},{1,2},{2,3},{3,0},{4,5},{5,6},{6,7},{7,4},{8,9},{9,10},{10,1... | collective-permute-start | bytes 9437192 | tf_op jit(solution)/shard_map/ppermute | solution.py:11
  150.7 61.5 %collective-permute-start.12 = (f32[8]{0:T(128)S(1)}, f32[8]{0:T(128)S(1)}, u32[]{:S(2)}, u32[]{:S(2)}) collective-permute-start(f32[8]{0:T(128)S(1)} %bitcast.86), channel_id=1, source_target_pairs={{0,28},{4,0},{8,4},{12,8},{16,12},{20,16},{24,20},{28,24},{1,29},{... | collective-permute-start | bytes 104 | tf_op jit(solution)/shard_map/ppermute | solution.py:11
  150.7 61.5 %collective-permute-start.24 = (f32[8]{0:T(128)S(1)}, f32[8]{0:T(128)S(1)}, u32[]{:S(2)}, u32[]{:S(2)}) collective-permute-start(f32[8]{0:T(128)S(1)} %bitcast.87), channel_id=1, source_target_pairs={{0,4},{4,8},{8,12},{12,16},{16,20},{20,24},{24,28},{28,0},{1,5},{5... | collective-permute-start | bytes 104 | tf_op jit(solution)/shard_map/ppermute | solution.py:11
  151.2 71.6 %collective-permute-start.4 = (f32[128]{0:T(128)S(1)}, f32[128]{0:T(128)S(1)}, u32[]{:S(2)}, u32[]{:S(2)}) collective-permute-start(f32[128]{0:T(128)S(1)} %bitcast.89), channel_id=1, source_target_pairs={{0,28},{4,0},{8,4},{12,8},{16,12},{20,16},{24,20},{28,24},{1,29},{... | collective-permute-start | bytes 1544 | tf_op jit(solution)/shard_map/ppermute | solution.py:11
  212.2 4.4 collective-permute-start.25
  214.8 3.5 collective-permute-start.13
  216.6 5.3 collective-permute-start.26
  218.4 5.2 collective-permute-start.14
  222.0 8.7 %collective-permute-start.27 = (f32[8]{0:T(128)S(1)}, f32[8]{0:T(128)S(1)}, u32[]{:S(2)}, u32[]{:S(2)}) collective-permute-start(f32[8]{0:T(128)S(1)} %broadcast_select_fusion.12), channel_id=1, source_target_pairs={{0,2},{1,3},{2,0},{3,1},{4,6},{5,7},{6,4},{7,5},{8,10},{9,11},{10,... | collective-permute-start | bytes 104 | tf_op jit(solution)/shard_map/ppermute | solution.py:11
  222.8 3.5 collective-permute-start.5
  223.6 146.0 %collective-permute-start.15 = (f32[8]{0:T(128)S(1)}, f32[8]{0:T(128)S(1)}, u32[]{:S(2)}, u32[]{:S(2)}) collective-permute-start(f32[8]{0:T(128)S(1)} %broadcast_select_fusion.13), channel_id=1, source_target_pairs={{0,2},{1,3},{2,0},{3,1},{4,6},{5,7},{6,4},{7,5},{8,10},{9,11},{10,... | collective-permute-start | bytes 104 | tf_op jit(solution)/shard_map/ppermute | solution.py:11
  226.3 4.3 collective-permute-start.6
  228.3 207.2 %collective-permute-start.2 = (f32[2,384,1024]{2,1,0:T(8,128)S(1)}, f32[2,384,1024]{2,1,0:T(8,128)S(1)}, u32[]{:S(2)}, u32[]{:S(2)}) collective-permute-start(f32[2,384,1024]{2,1,0:T(8,128)S(1)} %broadcast_select_fusion.3), channel_id=1, source_target_pairs={{0,3},{1,0},{2,1},{3,2},{4,7},{5,4},{6,5},{7,6},{8,11},{9,8},{10,9... | collective-permute-start | bytes 9437192 | tf_op jit(solution)/shard_map/ppermute | solution.py:11
  230.7 136.3 %collective-permute-start.7 = (f32[128]{0:T(128)S(1)}, f32[128]{0:T(128)S(1)}, u32[]{:S(2)}, u32[]{:S(2)}) collective-permute-start(f32[128]{0:T(128)S(1)} %broadcast_select_fusion.26), channel_id=1, source_target_pairs={{0,2},{1,3},{2,0},{3,1},{4,6},{5,7},{6,4},{7,5},{8,10},{9,11},{10,... | collective-permute-start | bytes 1544 | tf_op jit(solution)/shard_map/ppermute | solution.py:11
  233.0 206.6 %collective-permute-start.19 = (f32[2,384,1024]{2,1,0:T(8,128)S(1)}, f32[2,384,1024]{2,1,0:T(8,128)S(1)}, u32[]{:S(2)}, u32[]{:S(2)}) collective-permute-start(f32[2,384,1024]{2,1,0:T(8,128)S(1)} %broadcast_select_fusion.4), channel_id=1, source_target_pairs={{0,2},{1,3},{2,0},{3,1},{4,6},{5,7},{6,4},{7,5},{8,10},{9,11},{10,... | collective-permute-start | bytes 9437192 | tf_op jit(solution)/shard_map/ppermute | solution.py:11
  366.9 3.9 collective-permute-start.20
  366.9 3.9 collective-permute-start.8
  370.9 4.4 collective-permute-start.21
  372.7 3.5 collective-permute-start.9
  375.3 5.4 collective-permute-start.22
  376.2 57.7 %collective-permute-start.10 = (f32[128]{0:T(128)S(1)}, f32[128]{0:T(128)S(1)}, u32[]{:S(2)}, u32[]{:S(2)}) collective-permute-start(f32[128]{0:T(128)S(1)} %broadcast_select_fusion.19), channel_id=1, source_target_pairs={{0,3},{1,0},{2,1},{3,2},{4,7},{5,4},{6,5},{7,6},{8,11},{9,8},{10,9... | collective-permute-start | bytes 1544 | tf_op jit(solution)/shard_map/ppermute | solution.py:11
  380.7 54.8 %collective-permute-start.23 = (f32[128]{0:T(128)S(1)}, f32[128]{0:T(128)S(1)}, u32[]{:S(2)}, u32[]{:S(2)}) collective-permute-start(f32[128]{0:T(128)S(1)} %broadcast_select_fusion.20), channel_id=1, source_target_pairs={{0,2},{1,3},{2,0},{3,1},{4,6},{5,7},{6,4},{7,5},{8,10},{9,11},{10,... | collective-permute-start | bytes 1544 | tf_op jit(solution)/shard_map/ppermute | solution.py:11
  434.0 5.5 collective-permute-start.11
  436.5 137.2 %collective-permute-start.3 = (f32[2,384,1024]{2,1,0:T(8,128)S(1)}, f32[2,384,1024]{2,1,0:T(8,128)S(1)}, u32[]{:S(2)}, u32[]{:S(2)}) collective-permute-start(f32[2,384,1024]{2,1,0:T(8,128)S(1)} %broadcast_select_fusion.5), channel_id=1, source_target_pairs={{0,2},{1,3},{2,0},{3,1},{4,6},{5,7},{6,4},{7,5},{8,10},{9,11},{10,... | collective-permute-start | bytes 9437192 | tf_op jit(solution)/shard_map/ppermute | solution.py:11
  439.6 1.9 copy-start
where the time goes:
time: 651 us; the launch traced here: 646 us
  waiting for transfers between devices  432 us (66%)
  matrix products  100 us (15%)
  starting transfers between devices  94.5 us (15%)
  other arithmetic  11.4 us (2%)
    ppermute x28, waiting for transfers between devices, shifted(): return lax.ppermute(x, axis, [(i, (i + by) % size) for i in range(size)])  432 us
    ppermute x28, starting transfers between devices, shifted(): return lax.ppermute(x, axis, [(i, (i + by) % size) for i in range(size)])  94.5 us
    dot_general x8, matrix products, inner_first(): lax.dot_general(left, right, (((0,), (0,)), ((), ())), precision=lax.Prec...  57.4 us
    dot_general x4, matrix products, product(): jnp.dot(left, right, precision=lax.Precision.HIGHEST, preferred_element_t...  21.5 us
    dot_general x4, matrix products, inner_last(): lax.dot_general(left, right, (((1,), (1,)), ((), ())), precision=lax.Prec...  21.4 us
  transfers between devices with their start and end apart: 28, of which 15 were waited for; matrix products, arithmetic and copies ran while one was open for 6% of the time, Pallas kernels for 0%

commit v1 on v0

v1 whole, which is shorter than its diff:
```python
import jax
import jax.numpy as jnp
from jax import lax
from jax.sharding import PartitionSpec as P

REACH = 4
CHUNKS = 4
HIGH = lax.Precision.HIGH


def moved(x, by_x, by_z):
    count_x, count_z = lax.axis_size("kxy"), lax.axis_size("kz")
    pairs = []
    for at_x in range(count_x):
        for at_z in range(count_z):
            to_x, to_z = (at_x + by_x) % count_x, (at_z + by_z) % count_z
            pairs.append((at_x * count_z + at_z, to_x * count_z + to_z))
    return lax.ppermute(x, ("kxy", "kz"), pairs)


def shifted(x, axis, by):
    size = lax.axis_size(axis)
    return lax.ppermute(x, axis, [(i, (i + by) % size) for i in range(size)])


def dot(left, right, left_dim, right_dim):
    return lax.dot_general(
        left,
        right,
        (((left_dim,), (right_dim,)), ((), ())),
        precision=HIGH,
        preferred_element_type=jnp.float32,
    )


def amplitudes(first, second, gap_first, gap_second):
    real_v = dot(first[0], second[0], 0, 0) + dot(first[1], second[1], 0, 0)
    imag_v = dot(first[1], second[0], 0, 0) - dot(first[0], second[1], 0, 0)
    scale = 1.0 / (gap_first[:, None] + gap_second[None, :])
    return real_v * scale, imag_v * scale


def gaps(vir, occ):
    return (vir[None, :] - occ[:, None]).reshape(-1)


def body(factors, occ_energy, vir_energy, shifts):
    own = factors[0, 0]
    width = own.shape[2] // CHUNKS
    pieces = [own[:, :, c * width : (c + 1) * width] for c in range(CHUNKS)]
    partner = [moved(piece, 1 - REACH, 1 - REACH) for piece in pieces]
    behind = [moved(piece, REACH - 1, REACH - 1) for piece in pieces]
    vir_moved = vir_energy[0, 0]
    for axis, by in (("kxy", shifts[0, 0]), ("kz", shifts[0, 1])):
        for level in range((REACH - 1).bit_length()):
            arrived = shifted(vir_moved, axis, -(1 << level))
            vir_moved = jnp.where(by >> level & 1 == 1, arrived, vir_moved)
    levels = jnp.concatenate([vir_moved, occ_energy[0, 0]])
    ahead_levels = moved(levels, 1 - REACH, 1 - REACH)
    behind_levels = moved(levels, REACH - 1, REACH - 1)
    virs = vir_moved.shape[0]
    gap_own = gaps(vir_moved, occ_energy[0, 0])
    gap_ahead = gaps(ahead_levels[:virs], ahead_levels[virs:])
    gap_behind = gaps(behind_levels[:virs], behind_levels[virs:])
    real, imag = 0.0, 0.0
    for c in range(CHUNKS):
        here = slice(c * width, (c + 1) * width)
        part = partner[c]
        real_t, imag_t = amplitudes(own, part, gap_own, gap_ahead[here])
        real += dot(part[0], real_t, 1, 1) - dot(part[1], imag_t, 1, 1)
        imag += dot(part[0], imag_t, 1, 1) + dot(part[1], real_t, 1, 1)
        back = behind[c]
        real_t, imag_t = amplitudes(back, own, gap_behind[here], gap_own)
        real += dot(back[0], real_t, 1, 0) + dot(back[1], imag_t, 1, 0)
        imag += dot(back[1], real_t, 1, 0) - dot(back[0], imag_t, 1, 0)
    return -jnp.stack([real, imag])[None, None]


def solution(mesh):
    placed = (P("kxy", "kz", None, None, None), P("kxy", "kz", None), P("kxy", "kz", None), P())
    return jax.shard_map(
        body,
        mesh=mesh,
        in_specs=placed,
        out_specs=P("kxy", "kz", None, None, None),
        check_vma=False,
    )
```

time: 651 us -> 269 us (0.41)
  waiting for transfers between devices: 432 us -> 108 us
  starting transfers between devices: 94.5 us -> 28.4 us
  matrix products: 100 us -> 117 us
  other arithmetic: 11.4 us -> 1.1 us
    ppermute x28 -> x4, waiting for transfers between devices: 432 us -> 3.06 us  [shifted(): return lax.ppermute(x, axis, [(i, (i + by) % size) for i in range(size)])]
    ppermute x0 -> x10, waiting for transfers between devices: none -> 105 us  [moved(): return lax.ppermute(x, ('kxy', 'kz'), pairs)]
    ppermute x28 -> x4, starting transfers between devices: 94.5 us -> 8.73 us  [shifted(): return lax.ppermute(x, axis, [(i, (i + by) % size) for i in range(size)])]
    ppermute x0 -> x10, starting transfers between devices: none -> 19.7 us  [moved(): return lax.ppermute(x, ('kxy', 'kz'), pairs)]
    dot_general x16 -> x64, matrix products: 100 us -> 117 us  [dot(): lax.dot_general(left, right, (((left_dim,), (right_dim,)), ((), ())), pre...]
    select_n x25 -> x4, other arithmetic: 8.53 us -> 0.67 us  [body(): vir_moved = jnp.where(by >> level & 1 == 1, arrived, vir_moved)]
  transfers between devices with their start and end apart: 28 -> 14, of which waited for: 15 -> 6; matrix products, arithmetic and copies ran while one was open for 6% -> 8% of each run, Pallas kernels for 0% -> 0%
where the time goes in v1:
time: 269 us; the launch traced here: 264 us
  matrix products  117 us (43%)
  waiting for transfers between devices  108 us (40%)
  starting transfers between devices  28.4 us (11%)
  local copies, waits for them, and re-layouts  6.08 us (2%)
  between operations  3.37 us (1%)
    dot_general x64, matrix products, dot(): lax.dot_general(left, right, (((left_dim,), (right_dim,)), ((), ())), pre...  117 us
    ppermute x10, waiting for transfers between devices, moved(): return lax.ppermute(x, ('kxy', 'kz'), pairs)  105 us
    ppermute x10, starting transfers between devices, moved(): return lax.ppermute(x, ('kxy', 'kz'), pairs)  19.7 us
    ppermute x4, starting transfers between devices, shifted(): return lax.ppermute(x, axis, [(i, (i + by) % size) for i in range(size)])  8.73 us
  transfers between devices with their start and end apart: 14, of which 6 were waited for; matrix products, arithmetic and copies ran while one was open for 8% of the time, Pallas kernels for 0%

profile of v1, /device:TPU:0, one launch (start us, length us, event | category | flops | bytes accessed | tf_op | source)
XLA Modules:
  0.0 264.3 jit_solution(9399325138890406445)
XLA Ops:
  0.0 3.3 %collective-permute-start.1 = (f32[128]{0:T(128)}, f32[128]{0:T(128)S(1)}, u32[]{:S(2)}, u32[]{:S(2)}) collective-permute-start(f32[128]{0:T(128)} %bitcast.295), channel_id=1, source_target_pairs={{0,28},{4,0},{8,4},{12,8},{16,12},{20,16},{24,20},{28,24},{1,29},{... | collective-permute-start | bytes 1544 | tf_op jit(solution)/shard_map/ppermute | solution.py:23
  3.3 1.3 fusion.223
  7.0 2.4 collective-permute-done.2
  9.5 3.6 %collective-permute-start.3 = (f32[128]{0:T(128)S(1)}, f32[128]{0:T(128)S(1)}, u32[]{:S(2)}, u32[]{:S(2)}) collective-permute-start(f32[128]{0:T(128)S(1)} %broadcast_select_fusion.1), channel_id=1, source_target_pairs={{0,3},{1,0},{2,1},{3,2},{4,7},{5,4},{6,5},{7,6},{8,11},{9,8},{10,9... | collective-permute-start | bytes 1544 | tf_op jit(solution)/shard_map/ppermute | solution.py:23
  14.4 1.2 collective-permute-start.4
  15.6 2.3 fusion.222
  17.9 1.2 collective-permute-start
  19.1 3.3 %collective-permute-start.6 = (f32[2,384,256]{2,1,0:T(8,128)S(1)}, f32[2,384,256]{2,1,0:T(8,128)S(1)}, u32[]{:S(2)}, u32[]{:S(2)}) collective-permute-start(f32[2,384,256]{2,1,0:T(8,128)S(1)} %get-tuple-element.5), channel_id=1, source_target_pairs={{0,15},{1,12},{2,13},{3,14},{4,19},{5,16},{6,17},{7,18},{8,23},{9,... | collective-permute-start | bytes 2359304 | tf_op jit(solution)/shard_map/ppermute | solution.py:18
  23.1 2.0 collective-permute-start.5
  25.1 2.6 collective-permute-start.7
  27.8 46.1 %collective-permute-done.5 = f32[136]{0:T(256)S(1)} collective-permute-done((f32[136]{0:T(256)S(1)}, f32[136]{0:T(256)S(1)}, u32[]{:S(2)}, u32[]{:S(2)}) %collective-permute-start.5) | collective-permute-done | bytes 576 | tf_op jit(solution)/shard_map/ppermute | solution.py:18
  75.0 1.6 collective-permute-start.10
  76.8 2.9 %collective-permute-start.11 = (f32[2,384,256]{2,1,0:T(8,128)S(1)}, f32[2,384,256]{2,1,0:T(8,128)S(1)}, u32[]{:S(2)}, u32[]{:S(2)}) collective-permute-start(f32[2,384,256]{2,1,0:T(8,128)S(1)} %get-tuple-element.7), channel_id=1, source_target_pairs={{0,15},{1,12},{2,13},{3,14},{4,19},{5,16},{6,17},{7,18},{8,23},{9,... | collective-permute-start | bytes 2359304 | tf_op jit(solution)/shard_map/ppermute | solution.py:18
  79.7 1.4 fusion.30
  81.1 1.4 fusion.60
  84.9 4.9 %collective-permute-start.13 = (f32[2,384,256]{2,1,0:T(8,128)S(1)}, f32[2,384,256]{2,1,0:T(8,128)S(1)}, u32[]{:S(2)}, u32[]{:S(2)}) collective-permute-start(f32[2,384,256]{2,1,0:T(8,128)S(1)} %get-tuple-element.6), channel_id=1, source_target_pairs={{0,15},{1,12},{2,13},{3,14},{4,19},{5,16},{6,17},{7,18},{8,23},{9,... | collective-permute-start | bytes 2359304 | tf_op jit(solution)/shard_map/ppermute | solution.py:18
  89.9 1.4 fusion.22
  91.3 1.4 fusion.52
  92.8 18.5 %collective-permute-done.9 = f32[2,384,256]{2,1,0:T(8,128)S(1)} collective-permute-done((f32[2,384,256]{2,1,0:T(8,128)S(1)}, f32[2,384,256]{2,1,0:T(8,128)S(1)}, u32[]{:S(2)}, u32[]{:S(2)}) %collective-permute-start.9) | collective-permute-done | bytes 786464 | tf_op jit(solution)/shard_map/ppermute | solution.py:18
  113.5 1.4 fusion.14
  115.0 1.4 fusion.44
  116.4 28.5 %collective-permute-done.11 = f32[2,384,256]{2,1,0:T(8,128)S(1)} collective-permute-done((f32[2,384,256]{2,1,0:T(8,128)S(1)}, f32[2,384,256]{2,1,0:T(8,128)S(1)}, u32[]{:S(2)}, u32[]{:S(2)}) %collective-permute-start.11) | collective-permute-done | bytes 786464 | tf_op jit(solution)/shard_map/ppermute | solution.py:18
  147.2 1.4 fusion.6
  148.6 1.4 fusion.36
  150.1 11.9 %collective-permute-done.13 = f32[2,384,256]{2,1,0:T(8,128)S(1)} collective-permute-done((f32[2,384,256]{2,1,0:T(8,128)S(1)}, f32[2,384,256]{2,1,0:T(8,128)S(1)}, u32[]{:S(2)}, u32[]{:S(2)}) %collective-permute-start.13) | collective-permute-done | bytes 786464 | tf_op jit(solution)/shard_map/ppermute | solution.py:18
  162.0 1.3 fusion
  164.4 1.7 fusion.139
  168.1 1.6 fusion.67
  171.7 1.2 fusion.79
  172.9 1.9 fusion.167
  174.8 2.1 fusion.164
  176.9 1.2 fusion.73
  178.1 1.9 fusion.165
  179.9 1.9 fusion.166
  181.8 1.7 fusion.145
  185.5 1.6 fusion.85
  187.1 1.4 fusion.169
  190.7 1.9 fusion.175
  192.6 1.9 fusion.172
  194.5 1.2 fusion.91
  195.6 3.0 %fusion.173 = f32[1024,384]{1,0:T(8,128)} fusion(f32[256,1024]{1,0:T(8,128)S(1)} %fusion.91, f32[2,384,256]{2,1,0:T(8,128)S(1)} %collective-permute-done.9), kind=kOutput, calls=%fused_computation.136 | convolution fusion | flops 603979776 | bytes 3014656 | tf_op jit(solution)/shard_map/dot_general | solution.py:27
  198.7 1.9 fusion.174
  200.5 1.7 fusion.151
  202.2 2.3 fusion.179
  205.6 1.6 fusion.103
  207.2 2.2 fusion.177
  210.4 1.2 fusion.115
  211.6 3.0 %fusion.183 = f32[1024,384]{1,0:T(8,128)} fusion(f32[256,1024]{1,0:T(8,128)S(1)} %fusion.115, f32[2,384,256]{2,1,0:T(8,128)S(1)} %collective-permute-done.11), kind=kOutput, calls=%fused_computation.146 | convolution fusion | flops 603979776 | bytes 3014656 | tf_op jit(solution)/shard_map/dot_general | solution.py:27
  214.6 3.0 %fusion.180 = f32[1024,384]{1,0:T(8,128)} fusion(f32[256,1024]{1,0:T(8,128)S(1)} %fusion.115, f32[2,384,256]{2,1,0:T(8,128)S(1)} %collective-permute-done.11), kind=kOutput, calls=%fused_computation.143 | convolution fusion | flops 603979776 | bytes 3014656 | tf_op jit(solution)/shard_map/dot_general | solution.py:27
  218.8 3.2 %fusion.181 = f32[1024,384]{1,0:T(8,128)} fusion(f32[256,1024]{1,0:T(8,128)S(1)} %fusion.109, f32[2,384,256]{2,1,0:T(8,128)S(1)} %collective-permute-done.11), kind=kOutput, calls=%fused_computation.144 | convolution fusion | flops 603979776 | bytes 3014656 | tf_op jit(solution)/shard_map/dot_general | solution.py:27
  222.0 3.0 %fusion.182 = f32[1024,384]{1,0:T(8,128)} fusion(f32[256,1024]{1,0:T(8,128)S(1)} %fusion.109, f32[2,384,256]{2,1,0:T(8,128)S(1)} %collective-permute-done.11), kind=kOutput, calls=%fused_computation.145 | convolution fusion | flops 603979776 | bytes 3014656 | tf_op jit(solution)/shard_map/dot_general | solution.py:27
  225.0 1.6 fusion.121
  226.6 2.2 fusion.185
  228.7 2.1 fusion.186
  230.9 1.7 fusion.157
  232.6 2.1 fusion.187
  234.7 2.2 fusion.184
  236.9 1.2 fusion.133
  238.1 3.0 %fusion.189 = f32[1024,384]{1,0:T(8,128)} fusion(f32[256,1024]{1,0:T(8,128)S(1)} %fusion.133, f32[2,384,256]{2,1,0:T(8,128)S(1)} %collective-permute-done.13), kind=kOutput, calls=%fused_computation.152 | convolution fusion | flops 603979776 | bytes 3014656 | tf_op jit(solution)/shard_map/dot_general | solution.py:27
  241.1 3.2 %fusion.188 = f32[1024,384]{1,0:T(8,128)} fusion(f32[256,1024]{1,0:T(8,128)S(1)} %fusion.133, f32[2,384,256]{2,1,0:T(8,128)S(1)} %collective-permute-done.13), kind=kOutput, calls=%fused_computation.151 | convolution fusion | flops 603979776 | bytes 3014656 | tf_op jit(solution)/shard_map/dot_general | solution.py:27
  244.3 1.2 fusion.127
  245.5 9.1 %add_bitcast_fusion.1 = f32[1,1,1,384,1024]{3,4,2,1,0:T(8,128)} fusion(f32[1024,384]{1,0:T(8,128)} %fusion.189, f32[1024,384]{1,0:T(8,128)} %fusion.185, f32[1024,384]{1,0:T(8,128)} %fusion.187, f32[1024,384]{1,0:T(8,128)} %fusion.181, f32[1024,384]{1,0:T(8,128)} %fusion.183, f32[1024,384]{1,0:T(8,128)} %fusion.177, f32[1024,384]{1,0:T(8,128)} %fusion.179, ...), kind=kOutput, calls=%fused_computation.66 | convolution fusion | flops 609878016 | bytes 26607616 | tf_op jit(solution)/shard_map/dot_general | solution.py:27
  254.6 6.7 %add_bitcast_fusion = f32[1,1,1,384,1024]{3,4,2,1,0:T(8,128)S(1)} fusion(f32[1024,384]{1,0:T(8,128)} %fusion.188, f32[1024,384]{1,0:T(8,128)} %fusion.184, f32[1024,384]{1,0:T(8,128)} %fusion.186, f32[1024,384]{1,0:T(8,128)} %fusion.182, f32[1024,384]{1,0:T(8,128)} %fusion.180, f32[1024,384]{1,0:T(8,128)S(1)} %fusion.176, f32[1024,384]{1,0:T(8,128)S(1)} %fusion.178, ...), kind=kOutput, calls=%fused_computation.65 | convolution fusion | flops 609878016 | bytes 26607616 | tf_op jit(solution)/shard_map/dot_general | solution.py:27
  261.5 2.4 copy.5
  (52 shorter events, 22.6 us)
Async XLA Ops:
  0.0 5.2 %collective-permute-start.1 = (f32[128]{0:T(128)}, f32[128]{0:T(128)S(1)}, u32[]{:S(2)}, u32[]{:S(2)}) collective-permute-start(f32[128]{0:T(128)} %bitcast.295), channel_id=1, source_target_pairs={{0,28},{4,0},{8,4},{12,8},{16,12},{20,16},{24,20},{28,24},{1,29},{... | collective-permute-start | bytes 1544 | tf_op jit(solution)/shard_map/ppermute | solution.py:23
  5.9 3.5 %collective-permute-start.2 = (f32[128]{0:T(128)S(1)}, f32[128]{0:T(128)S(1)}, u32[]{:S(2)}, u32[]{:S(2)}) collective-permute-start(f32[128]{0:T(128)S(1)} %broadcast_select_fusion), channel_id=1, source_target_pairs={{0,24},{4,28},{8,0},{12,4},{16,8},{20,12},{24,16},{28,20},{1,25},{... | collective-permute-start | bytes 1544 | tf_op jit(solution)/shard_map/ppermute | solution.py:23
  9.5 4.9 %collective-permute-start.3 = (f32[128]{0:T(128)S(1)}, f32[128]{0:T(128)S(1)}, u32[]{:S(2)}, u32[]{:S(2)}) collective-permute-start(f32[128]{0:T(128)S(1)} %broadcast_select_fusion.1), channel_id=1, source_target_pairs={{0,3},{1,0},{2,1},{3,2},{4,7},{5,4},{6,5},{7,6},{8,11},{9,8},{10,9... | collective-permute-start | bytes 1544 | tf_op jit(solution)/shard_map/ppermute | solution.py:23
  14.4 8.7 %collective-permute-start.4 = (f32[128]{0:T(128)S(1)}, f32[128]{0:T(128)S(1)}, u32[]{:S(2)}, u32[]{:S(2)}) collective-permute-start(f32[128]{0:T(128)S(1)} %broadcast_select_fusion.2), channel_id=1, source_target_pairs={{0,2},{1,3},{2,0},{3,1},{4,6},{5,7},{6,4},{7,5},{8,10},{9,11},{10,... | collective-permute-start | bytes 1544 | tf_op jit(solution)/shard_map/ppermute | solution.py:23
  15.6 7.5 %copy-start.2 = (f32[1,1,8]{2,1,0:T(1,128)S(1)}, f32[1,1,8]{2,1,0:T(1,128)}, u32[]{:S(2)}) copy-start(f32[1,1,8]{2,1,0:T(1,128)} %param.5) | copy-start | bytes 100
  15.6 64.1 %copy-start = (f32[1,1,2,384,1024]{4,3,2,1,0:T(8,128)S(1)}, f32[1,1,2,384,1024]{4,3,2,1,0:T(8,128)}, u32[]{:S(2)}) copy-start(f32[1,1,2,384,1024]{4,3,2,1,0:T(8,128)} %param.4) | copy-start | bytes 9437188
  17.9 58.8 %collective-permute-start = (f32[2,384,256]{2,1,0:T(8,128)S(1)}, f32[2,384,256]{2,1,0:T(8,128)S(1)}, u32[]{:S(2)}, u32[]{:S(2)}) collective-permute-start(f32[2,384,256]{2,1,0:T(8,128)S(1)} %get-tuple-element.5), channel_id=1, source_target_pairs={{0,21},{1,22},{2,23},{3,20},{4,25},{5,26},{6,27},{7,24},{8,29},{9,... | collective-permute-start | bytes 2359304 | tf_op jit(solution)/shard_map/ppermute | solution.py:18
  19.1 63.5 %collective-permute-start.6 = (f32[2,384,256]{2,1,0:T(8,128)S(1)}, f32[2,384,256]{2,1,0:T(8,128)S(1)}, u32[]{:S(2)}, u32[]{:S(2)}) collective-permute-start(f32[2,384,256]{2,1,0:T(8,128)S(1)} %get-tuple-element.5), channel_id=1, source_target_pairs={{0,15},{1,12},{2,13},{3,14},{4,19},{5,16},{6,17},{7,18},{8,23},{9,... | collective-permute-start | bytes 2359304 | tf_op jit(solution)/shard_map/ppermute | solution.py:18
  22.4 62.5 %collective-permute-start.8 = (f32[2,384,256]{2,1,0:T(8,128)S(1)}, f32[2,384,256]{2,1,0:T(8,128)S(1)}, u32[]{:S(2)}, u32[]{:S(2)}) collective-permute-start(f32[2,384,256]{2,1,0:T(8,128)S(1)} %get-tuple-element.8), channel_id=1, source_target_pairs={{0,21},{1,22},{2,23},{3,20},{4,25},{5,26},{6,27},{7,24},{8,29},{9,... | collective-permute-start | bytes 2359304 | tf_op jit(solution)/shard_map/ppermute | solution.py:18
  23.1 50.7 %collective-permute-start.5 = (f32[136]{0:T(256)S(1)}, f32[136]{0:T(256)S(1)}, u32[]{:S(2)}, u32[]{:S(2)}) collective-permute-start(f32[136]{0:T(256)S(1)} %pad_maximum_fusion), channel_id=1, source_target_pairs={{0,21},{1,22},{2,23},{3,20},{4,25},{5,26},{6,27},{7,24},{8,29},{9,... | collective-permute-start | bytes 1640 | tf_op jit(solution)/shard_map/ppermute | solution.py:18
  25.1 49.9 %collective-permute-start.7 = (f32[136]{0:T(256)S(1)}, f32[136]{0:T(256)S(1)}, u32[]{:S(2)}, u32[]{:S(2)}) collective-permute-start(f32[136]{0:T(256)S(1)} %pad_maximum_fusion), channel_id=1, source_target_pairs={{0,15},{1,12},{2,13},{3,14},{4,19},{5,16},{6,17},{7,18},{8,23},{9,... | collective-permute-start | bytes 1640 | tf_op jit(solution)/shard_map/ppermute | solution.py:18
  73.9 37.4 %collective-permute-start.9 = (f32[2,384,256]{2,1,0:T(8,128)S(1)}, f32[2,384,256]{2,1,0:T(8,128)S(1)}, u32[]{:S(2)}, u32[]{:S(2)}) collective-permute-start(f32[2,384,256]{2,1,0:T(8,128)S(1)} %get-tuple-element.8), channel_id=1, source_target_pairs={{0,15},{1,12},{2,13},{3,14},{4,19},{5,16},{6,17},{7,18},{8,23},{9,... | collective-permute-start | bytes 2359304 | tf_op jit(solution)/shard_map/ppermute | solution.py:18
  75.0 38.6 %collective-permute-start.10 = (f32[2,384,256]{2,1,0:T(8,128)S(1)}, f32[2,384,256]{2,1,0:T(8,128)S(1)}, u32[]{:S(2)}, u32[]{:S(2)}) collective-permute-start(f32[2,384,256]{2,1,0:T(8,128)S(1)} %get-tuple-element.7), channel_id=1, source_target_pairs={{0,21},{1,22},{2,23},{3,20},{4,25},{5,26},{6,27},{7,24},{8,29},{9,... | collective-permute-start | bytes 2359304 | tf_op jit(solution)/shard_map/ppermute | solution.py:18
  76.8 68.2 %collective-permute-start.11 = (f32[2,384,256]{2,1,0:T(8,128)S(1)}, f32[2,384,256]{2,1,0:T(8,128)S(1)}, u32[]{:S(2)}, u32[]{:S(2)}) collective-permute-start(f32[2,384,256]{2,1,0:T(8,128)S(1)} %get-tuple-element.7), channel_id=1, source_target_pairs={{0,15},{1,12},{2,13},{3,14},{4,19},{5,16},{6,17},{7,18},{8,23},{9,... | collective-permute-start | bytes 2359304 | tf_op jit(solution)/shard_map/ppermute | solution.py:18
  82.6 64.6 %collective-permute-start.12 = (f32[2,384,256]{2,1,0:T(8,128)S(1)}, f32[2,384,256]{2,1,0:T(8,128)S(1)}, u32[]{:S(2)}, u32[]{:S(2)}) collective-permute-start(f32[2,384,256]{2,1,0:T(8,128)S(1)} %get-tuple-element.6), channel_id=1, source_target_pairs={{0,21},{1,22},{2,23},{3,20},{4,25},{5,26},{6,27},{7,24},{8,29},{9,... | collective-permute-start | bytes 2359304 | tf_op jit(solution)/shard_map/ppermute | solution.py:18
  84.9 77.1 %collective-permute-start.13 = (f32[2,384,256]{2,1,0:T(8,128)S(1)}, f32[2,384,256]{2,1,0:T(8,128)S(1)}, u32[]{:S(2)}, u32[]{:S(2)}) collective-permute-start(f32[2,384,256]{2,1,0:T(8,128)S(1)} %get-tuple-element.6), channel_id=1, source_target_pairs={{0,15},{1,12},{2,13},{3,14},{4,19},{5,16},{6,17},{7,18},{8,23},{9,... | collective-permute-start | bytes 2359304 | tf_op jit(solution)/shard_map/ppermute | solution.py:18
  254.6 6.7 %copy-start.1 = (f32[1,1,1,384,1024]{3,4,2,1,0:T(8,128)S(1)}, f32[1,1,1,384,1024]{3,4,2,1,0:T(8,128)}, u32[]{:S(2)}) copy-start(f32[1,1,1,384,1024]{3,4,2,1,0:T(8,128)} %add_bitcast_fusion.1) | copy-start | bytes 4718596

commit v2 on v1

v2 whole, which is shorter than its diff:
```python
import functools

import jax
import jax.numpy as jnp
from jax import lax
from jax.experimental import pallas as pl
from jax.experimental.pallas import tpu as pltpu
from jax.sharding import PartitionSpec as P

REACH = 4
WINDOW = 2
TILE = 256
MESH = pl.DeviceIdType.MESH


def halves(x):
    high = x.astype(jnp.bfloat16)
    return high, (x - high.astype(jnp.float32)).astype(jnp.bfloat16)


def dot(left, right):
    return jnp.dot(left, right, preferred_element_type=jnp.float32)


def three_pass(left, right):
    return dot(left[0], right[0]) + dot(left[0], right[1]) + dot(left[1], right[0])


def offsets(size_x, size_z):
    reach = range(1, REACH)
    found = set()
    for sign in (1, -1):
        found.update((sign * s % size_x, 0) for s in reach)
        found.update((0, sign * s % size_z) for s in reach)
        found.add((sign * (REACH - 1) % size_x, sign * (REACH - 1) % size_z))
    return sorted(found)


def kernel(
    size_x, size_z, shifts_ref, panel_ref, vir_ref, occ_ref, out_ref,
    landed, own_f32, own_split, mixed, mixed_t, vir_x, vir_step, vir_z, gap_own, gap_landed, gap_column,
    load_sem, send_sem, recv_sem, hop_send, hop_recv, gap_send, gap_recv,
):
    at_x, at_z = lax.axis_index("kxy"), lax.axis_index("kz")
    naux = panel_ref.shape[1]
    occs, virs = occ_ref.shape
    step = REACH - 1

    load = pltpu.make_async_copy(panel_ref, own_f32, load_sem)
    load.start()

    def device(by_x, by_z):
        return (lax.rem(at_x + by_x + size_x * REACH, size_x), lax.rem(at_z + by_z + size_z * REACH, size_z))

    barrier = pltpu.get_barrier_semaphore()
    greeted = offsets(size_x, size_z)
    for by_x, by_z in greeted:
        pl.semaphore_signal(barrier, inc=1, device_id=device(by_x, by_z), device_id_type=MESH)
    pl.semaphore_wait(barrier, len(greeted))

    def hop(source, slots, axis, s):
        return pltpu.make_async_remote_copy(
            src_ref=source,
            dst_ref=slots.at[s - 1],
            send_sem=hop_send.at[axis, s - 1],
            recv_sem=hop_recv.at[axis, s - 1],
            device_id=device(-s, 0) if axis == 0 else device(0, -s),
            device_id_type=MESH,
        )

    def block_copy(way, c):
        sign = 2 * way - 1
        columns = pl.ds(pl.multiple_of(c * virs, virs), virs)
        return pltpu.make_async_remote_copy(
            src_ref=panel_ref.at[:, :, columns],
            dst_ref=landed.at[way, :, :, columns],
            send_sem=send_sem.at[way, c],
            recv_sem=recv_sem.at[way, c],
            device_id=device(sign * step, sign * step),
            device_id_type=MESH,
        )

    def gap_copy(way):
        sign = 2 * way - 1
        return pltpu.make_async_remote_copy(
            src_ref=gap_own,
            dst_ref=gap_landed.at[way],
            send_sem=gap_send.at[way],
            recv_sem=gap_recv.at[way],
            device_id=device(sign * step, sign * step),
            device_id_type=MESH,
        )

    for s in range(1, REACH):
        hop(vir_ref, vir_x, 0, s).start()
    for c in range(WINDOW):
        for way in range(2):
            block_copy(way, c).start()

    def chosen(slots, by):
        picked = slots[0]
        for s in range(2, REACH):
            picked = jnp.where(by == s, slots[s - 1], picked)
        return picked

    for s in range(1, REACH):
        hop(vir_ref, vir_x, 0, s).wait()
    vir_step[...] = chosen(vir_x, shifts_ref[0, 0])
    for s in range(1, REACH):
        hop(vir_step, vir_z, 1, s).start()
    load.wait()
    for part in range(2):
        rows = pl.ds(part * naux, naux)
        for at in range(0, own_split.shape[2], TILE):
            high, low = halves(own_f32[part, :, at : at + TILE])
            own_split[0, rows, at : at + TILE] = high
            own_split[1, rows, at : at + TILE] = low
    out_ref[...] = jnp.zeros_like(out_ref)
    for s in range(1, REACH):
        hop(vir_step, vir_z, 1, s).wait()
    gap_own[...] = chosen(vir_z, shifts_ref[0, 1]) - occ_ref[...]
    for way in range(2):
        gap_copy(way).start()
    for way in range(2):
        gap_copy(way).wait()
        for i in range(occs):
            row = gap_landed[way, i : i + 1, :]
            gap_column[way, i] = jnp.broadcast_to(row, (virs, virs)).T

    def work(at, carry):
        c, way = lax.div(at, 2), lax.rem(at, 2)

        @pl.when(way == 0)
        def _():
            for each in range(2):
                block_copy(each, c).wait_send()

            @pl.when(c + WINDOW < occs)
            def _():
                for each in range(2):
                    block_copy(each, c + WINDOW).start()

        block_copy(way, c).wait_recv()
        columns = pl.ds(pl.multiple_of(c * virs, virs), virs)
        real = landed[way, 0, :, columns]
        imag = landed[way, 1, :, columns]
        for which, (r, i) in enumerate(zip(halves(real), halves(imag))):
            mixed[which, :naux, :virs] = r
            mixed[which, :naux, virs:] = -i
            mixed[which, naux:, :virs] = i
            mixed[which, naux:, virs:] = r
        for which, (r, i) in enumerate(zip(halves(real.T), halves(imag.T))):
            mixed_t[which, :virs, :naux] = r
            mixed_t[which, :virs, naux:] = i
            mixed_t[which, virs:, :naux] = -i
            mixed_t[which, virs:, naux:] = r
        column_gap = gap_column[way, c]
        for start in range(0, occs * virs, TILE):
            tile = slice(start, start + TILE)
            v = three_pass((mixed_t[0], mixed_t[1]), (own_split[0, :, tile], own_split[1, :, tile]))
            scale = jnp.concatenate(
                [1.0 / (column_gap + gap_own[j : j + 1, :]) for j in range(start // virs, (start + TILE) // virs)], 1
            )
            t = halves(v * jnp.concatenate([scale, scale], 0))
            out_ref[:, tile] += three_pass((mixed[0], mixed[1]), t)
        return carry

    lax.fori_loop(0, 2 * occs, work, 0)


def body(factors, occ_energy, vir_energy, shifts):
    size_x, size_z = lax.axis_size("kxy"), lax.axis_size("kz")
    panel = factors[0, 0]
    parts, naux, pairs = panel.shape
    occs, virs = occ_energy.shape[2], vir_energy.shape[2]
    vir_rows = jnp.broadcast_to(vir_energy[0, 0][None, :], (occs, virs))
    occ_rows = jnp.broadcast_to(occ_energy[0, 0][:, None], (occs, virs))
    f32, bf16, dma = jnp.float32, jnp.bfloat16, pltpu.SemaphoreType.DMA
    vmem = pl.BlockSpec(memory_space=pltpu.VMEM)
    total = pl.pallas_call(
        functools.partial(kernel, size_x, size_z),
        out_shape=jax.ShapeDtypeStruct((parts * naux, pairs), f32),
        in_specs=[pl.BlockSpec(memory_space=pltpu.SMEM), pl.BlockSpec(memory_space=pl.ANY), vmem, vmem],
        out_specs=vmem,
        scratch_shapes=[
            pltpu.VMEM((2, parts, naux, pairs), f32),
            pltpu.VMEM((parts, naux, pairs), f32),
            pltpu.VMEM((2, parts * naux, pairs), bf16),
            pltpu.VMEM((2, parts * naux, 2 * virs), bf16),
            pltpu.VMEM((2, 2 * virs, parts * naux), bf16),
            pltpu.VMEM((REACH - 1, occs, virs), f32),
            pltpu.VMEM((occs, virs), f32),
            pltpu.VMEM((REACH - 1, occs, virs), f32),
            pltpu.VMEM((occs, virs), f32),
            pltpu.VMEM((2, occs, virs), f32),
            pltpu.VMEM((2, occs, virs, virs), f32),
            dma,
            dma((2, occs)),
            dma((2, occs)),
            dma((2, REACH - 1)),
            dma((2, REACH - 1)),
            dma((2,)),
            dma((2,)),
        ],
        compiler_params=pltpu.CompilerParams(
            collective_id=0, has_side_effects=True, vmem_limit_bytes=48 * 1024 * 1024
        ),
        cost_estimate=pl.CostEstimate(
            flops=48 * naux * pairs * pairs, bytes_accessed=8 * panel.size, transcendentals=0
        ),
    )(shifts, panel, vir_rows, occ_rows)
    return -total.reshape(1, 1, parts, naux, pairs)


def solution(mesh):
    placed = (P("kxy", "kz", None, None, None), P("kxy", "kz", None), P("kxy", "kz", None), P())
    return jax.shard_map(
        body,
        mesh=mesh,
        in_specs=placed,
        out_specs=P("kxy", "kz", None, None, None),
        check_vma=False,
    )
```

time: 269 us -> 161 us (0.60); the launches traced: 264 us -> 161 us
  Pallas kernels: 0 us -> 157 us
  matrix products: 117 us -> 0 us
  waiting for transfers between devices: 108 us -> 0 us
  starting transfers between devices: 28.4 us -> 0 us
  local copies, waits for them, and re-layouts: 6.08 us -> 2.06 us
  between operations: 3.37 us -> 0.01 us
    pallas_call x0 -> x1, Pallas kernels: none -> 157 us  [body(): pl.pallas_call(functools.partial(kernel, size_x, size_z), out_shape=jax.S...]
    dot_general x64 -> x0, matrix products: 117 us -> none  [dot(): lax.dot_general(left, right, (((left_dim,), (right_dim,)), ((), ())), pre...]
    ppermute x14 -> x0, waiting for transfers between devices: 108 us -> none  [the longest x10 105 us: moved(): return lax.ppermute(x, ('kxy', 'kz'), pairs)]
    ppermute x14 -> x0, starting transfers between devices: 28.4 us -> none  [the longest x10 19.7 us: moved(): return lax.ppermute(x, ('kxy', 'kz'), pairs)]
    slice x6 -> x0, local copies, waits for them, and re-layouts: 3.7 us -> none  [the longest x1 2.35 us: body(): pieces = [own[:, :, c * width:(c + 1) * width] for c in range(CHUNKS)]]
  transfers between devices with their start and end apart: 14 -> 0, of which waited for: 6 -> 0; matrix products, arithmetic and copies ran while one was open for 8% -> 0% of each run, Pallas kernels for 0% -> 0%
where the time goes in v2:
time: 161 us
  Pallas kernels  157 us (98%)
  local copies, waits for them, and re-layouts  2.06 us (1%)
  other arithmetic  1.97 us (1%)
    pallas_call x1, Pallas kernels, body(): pl.pallas_call(functools.partial(kernel, size_x, size_z), out_shape=jax.S...  157 us

profile of v2, /device:TPU:0, one launch (start us, length us, event | category | flops | bytes accessed | tf_op | source)
XLA Modules:
  0.0 160.7 jit_solution(15773247486462340860)
XLA Ops:
  0.0 0.7 broadcast_in_dim.17.occ_ref
  0.7 0.7 broadcast_in_dim.15.vir_ref
  1.4 0.0 copy-start
  1.4 0.7 copy-done
  2.1 156.7 %shard_map.46 = f32[768,1024]{1,0:T(8,128)S(1)} custom-call(s32[2,2]{1,0:T(2,128)S(1)} %copy-done, f32[2,384,1024]{2,1,0:T(8,128)} %bitcast.6, f32[8,128]{1,0:T(8,128)S(1)} %broadcast_in_dim.15.vir_ref, f32[8,128]{1,0:T(8,128)S(1)} %broadcast_in_dim.17.occ_ref), custom_call_target="tpu_custom_call" | custom-call | flops 19327352832 | bytes 6291456 | tf_op jit(solution)/shard_map/pallas_call | solution.py:180
  158.7 2.0 %neg.14 = f32[768,1024]{1,0:T(8,128)} negate(f32[768,1024]{1,0:T(8,128)S(1)} %shard_map.46) | non-fusion elementwise | flops 786432 | bytes 6291456 | tf_op jit(solution)/shard_map/neg | solution.py:212
Async XLA Ops:
  1.4 0.7 copy-start

commit v3 on v2

--- a/solution.py
+++ b/solution.py
@@ -38,16 +38,20 @@
 
 def kernel(
     size_x, size_z, shifts_ref, panel_ref, vir_ref, occ_ref, out_ref,
-    landed, own_f32, own_split, mixed, mixed_t, vir_x, vir_step, vir_z, gap_own, gap_landed, gap_column,
+    landed, own_f32, own_split, mixed, mixed_t, vir_own, vir_x, vir_step, vir_z, gap_own, gap_landed, gap_column,
     load_sem, send_sem, recv_sem, hop_send, hop_recv, gap_send, gap_recv,
 ):
     at_x, at_z = lax.axis_index("kxy"), lax.axis_index("kz")
     naux = panel_ref.shape[1]
-    occs, virs = occ_ref.shape
+    occs, virs = gap_own.shape
     step = REACH - 1
 
-    load = pltpu.make_async_copy(panel_ref, own_f32, load_sem)
-    load.start()
+    def load(c):
+        return pltpu.make_async_copy(panel_ref.at[:, :, c * virs : (c + 1) * virs], own_f32.at[c], load_sem.at[c])
+
+    for c in range(occs):
+        load(c).start()
+    vir_own[...] = jnp.broadcast_to(vir_ref[...], (occs, virs))
 
     def device(by_x, by_z):
         return (lax.rem(at_x + by_x + size_x * REACH, size_x), lax.rem(at_z + by_z + size_z * REACH, size_z))
@@ -70,10 +74,9 @@
 
     def block_copy(way, c):
         sign = 2 * way - 1
-        columns = pl.ds(pl.multiple_of(c * virs, virs), virs)
         return pltpu.make_async_remote_copy(
-            src_ref=panel_ref.at[:, :, columns],
-            dst_ref=landed.at[way, :, :, columns],
+            src_ref=own_f32.at[c],
+            dst_ref=landed.at[way, c],
             send_sem=send_sem.at[way, c],
             recv_sem=recv_sem.at[way, c],
             device_id=device(sign * step, sign * step),
@@ -92,8 +95,9 @@
         )
 
     for s in range(1, REACH):
-        hop(vir_ref, vir_x, 0, s).start()
+        hop(vir_own, vir_x, 0, s).start()
     for c in range(WINDOW):
+        load(c).wait()
         for way in range(2):
             block_copy(way, c).start()
 
@@ -104,21 +108,25 @@
         return picked
 
     for s in range(1, REACH):
-        hop(vir_ref, vir_x, 0, s).wait()
+        hop(vir_own, vir_x, 0, s).wait()
     vir_step[...] = chosen(vir_x, shifts_ref[0, 0])
     for s in range(1, REACH):
         hop(vir_step, vir_z, 1, s).start()
-    load.wait()
-    for part in range(2):
-        rows = pl.ds(part * naux, naux)
-        for at in range(0, own_split.shape[2], TILE):
-            high, low = halves(own_f32[part, :, at : at + TILE])
-            own_split[0, rows, at : at + TILE] = high
-            own_split[1, rows, at : at + TILE] = low
+    for c in range(WINDOW, occs):
+        load(c).wait()
+    for c in range(occs):
+        columns = slice(c * virs, (c + 1) * virs)
+        for part in range(2):
+            rows = slice(part * naux, (part + 1) * naux)
+            high, low = halves(own_f32[c, part])
+            own_split[0, rows, columns] = high
+            own_split[1, rows, columns] = low
     out_ref[...] = jnp.zeros_like(out_ref)
     for s in range(1, REACH):
         hop(vir_step, vir_z, 1, s).wait()
-    gap_own[...] = chosen(vir_z, shifts_ref[0, 1]) - occ_ref[...]
+    vir_used = chosen(vir_z, shifts_ref[0, 1])
+    for i in range(occs):
+        gap_own[i : i + 1, :] = vir_used[i : i + 1, :] - occ_ref[0, i]
     for way in range(2):
         gap_copy(way).start()
     for way in range(2):
@@ -141,9 +149,8 @@
                     block_copy(each, c + WINDOW).start()
 
         block_copy(way, c).wait_recv()
-        columns = pl.ds(pl.multiple_of(c * virs, virs), virs)
-        real = landed[way, 0, :, columns]
-        imag = landed[way, 1, :, columns]
+        real = landed[way, c, 0]
+        imag = landed[way, c, 1]
         for which, (r, i) in enumerate(zip(halves(real), halves(imag))):
             mixed[which, :naux, :virs] = r
             mixed[which, :naux, virs:] = -i
@@ -173,28 +180,28 @@
     panel = factors[0, 0]
     parts, naux, pairs = panel.shape
     occs, virs = occ_energy.shape[2], vir_energy.shape[2]
-    vir_rows = jnp.broadcast_to(vir_energy[0, 0][None, :], (occs, virs))
-    occ_rows = jnp.broadcast_to(occ_energy[0, 0][:, None], (occs, virs))
     f32, bf16, dma = jnp.float32, jnp.bfloat16, pltpu.SemaphoreType.DMA
+    smem = pl.BlockSpec(memory_space=pltpu.SMEM)
     vmem = pl.BlockSpec(memory_space=pltpu.VMEM)
     total = pl.pallas_call(
         functools.partial(kernel, size_x, size_z),
         out_shape=jax.ShapeDtypeStruct((parts * naux, pairs), f32),
-        in_specs=[pl.BlockSpec(memory_space=pltpu.SMEM), pl.BlockSpec(memory_space=pl.ANY), vmem, vmem],
+        in_specs=[smem, pl.BlockSpec(memory_space=pl.ANY), vmem, smem],
         out_specs=vmem,
         scratch_shapes=[
-            pltpu.VMEM((2, parts, naux, pairs), f32),
-            pltpu.VMEM((parts, naux, pairs), f32),
+            pltpu.VMEM((2, occs, parts, naux, virs), f32),
+            pltpu.VMEM((occs, parts, naux, virs), f32),
             pltpu.VMEM((2, parts * naux, pairs), bf16),
             pltpu.VMEM((2, parts * naux, 2 * virs), bf16),
             pltpu.VMEM((2, 2 * virs, parts * naux), bf16),
+            pltpu.VMEM((occs, virs), f32),
             pltpu.VMEM((REACH - 1, occs, virs), f32),
             pltpu.VMEM((occs, virs), f32),
             pltpu.VMEM((REACH - 1, occs, virs), f32),
             pltpu.VMEM((occs, virs), f32),
             pltpu.VMEM((2, occs, virs), f32),
             pltpu.VMEM((2, occs, virs, virs), f32),
-            dma,
+            dma((occs,)),
             dma((2, occs)),
             dma((2, occs)),
             dma((2, REACH - 1)),
@@ -208,7 +215,7 @@
         cost_estimate=pl.CostEstimate(
             flops=48 * naux * pairs * pairs, bytes_accessed=8 * panel.size, transcendentals=0
         ),
-    )(shifts, panel, vir_rows, occ_rows)
+    )(shifts, panel, vir_energy[0], occ_energy[0])
     return -total.reshape(1, 1, parts, naux, pairs)
 
 

time: 161 us -> 160 us (level)
  no operation moved by 1% of the time
where the time goes in v3:
time: 160 us
  Pallas kernels  156 us (98%)
  local copies, waits for them, and re-layouts  1.99 us (1%)
  other arithmetic  1.97 us (1%)
    pallas_call x1, Pallas kernels, body(): pl.pallas_call(functools.partial(kernel, size_x, size_z), out_shape=jax.S...  156 us

profile of v3, /device:TPU:0, one launch (start us, length us, event | category | flops | bytes accessed | tf_op | source)
XLA Modules:
  0.0 160.2 jit_solution(6552156037800918140)
XLA Ops:
  0.0 0.0 copy-start
  0.0 0.7 copy-done
  0.7 0.0 copy-start.1
  0.7 0.7 copy-done.1
  1.3 0.0 copy-start.2
  1.3 0.7 copy-done.2
  2.0 156.3 %shard_map.46 = f32[768,1024]{1,0:T(8,128)S(1)} custom-call(s32[2,2]{1,0:T(2,128)S(1)} %copy-done, f32[2,384,1024]{2,1,0:T(8,128)} %bitcast.6, f32[1,128]{1,0:T(1,128)S(1)} %bitcast.4, f32[1,8]{1,0:T(1,128)S(1)} %bitcast.5), custom_call_target="tpu_custom_call" | custom-call | flops 19327352832 | bytes 6291456 | tf_op jit(solution)/shard_map/pallas_call | solution.py:186
  158.3 2.0 %neg.14 = f32[768,1024]{1,0:T(8,128)} negate(f32[768,1024]{1,0:T(8,128)S(1)} %shard_map.46) | non-fusion elementwise | flops 786432 | bytes 6291456 | tf_op jit(solution)/shard_map/neg | solution.py:219
Async XLA Ops:
  0.0 0.7 copy-start
  0.7 0.7 copy-start.1
  1.3 0.7 copy-start.2

commit v4 on v3

--- a/solution.py
+++ b/solution.py
@@ -98,8 +98,7 @@
         hop(vir_own, vir_x, 0, s).start()
     for c in range(WINDOW):
         load(c).wait()
-        for way in range(2):
-            block_copy(way, c).start()
+        block_copy(0, c).start()
 
     def chosen(slots, by):
         picked = slots[0]
@@ -129,6 +128,8 @@
         gap_own[i : i + 1, :] = vir_used[i : i + 1, :] - occ_ref[0, i]
     for way in range(2):
         gap_copy(way).start()
+    for c in range(WINDOW):
+        block_copy(1, c).start()
     for way in range(2):
         gap_copy(way).wait()
         for i in range(occs):
@@ -138,15 +139,11 @@
     def work(at, carry):
         c, way = lax.div(at, 2), lax.rem(at, 2)
 
-        @pl.when(way == 0)
+        block_copy(way, c).wait_send()
+
+        @pl.when(c + WINDOW < occs)
         def _():
-            for each in range(2):
-                block_copy(each, c).wait_send()
-
-            @pl.when(c + WINDOW < occs)
-            def _():
-                for each in range(2):
-                    block_copy(each, c + WINDOW).start()
+            block_copy(way, c + WINDOW).start()
 
         block_copy(way, c).wait_recv()
         real = landed[way, c, 0]

time: 160 us -> 154 us (0.963); the launches traced: 160 us -> 152 us
  Pallas kernels: 156 us -> 148 us
    pallas_call x1, Pallas kernels: 156 us -> 148 us  [body(): pl.pallas_call(functools.partial(kernel, size_x, size_z), out_shape=jax.S...]
where the time goes in v4:
time: 154 us; the launch traced here: 152 us
  Pallas kernels  148 us (96%)
  local copies, waits for them, and re-layouts  1.99 us (1%)
  other arithmetic  1.97 us (1%)
    pallas_call x1, Pallas kernels, body(): pl.pallas_call(functools.partial(kernel, size_x, size_z), out_shape=jax.S...  148 us

profile of v4, /device:TPU:0, one launch (start us, length us, event | category | flops | bytes accessed | tf_op | source)
XLA Modules:
  0.0 152.3 jit_solution(17113965472824351133)
XLA Ops:
  0.0 0.0 copy-start
  0.0 0.7 copy-done
  0.7 0.0 copy-start.1
  0.7 0.7 copy-done.1
  1.3 0.0 copy-start.2
  1.3 0.7 copy-done.2
  2.0 148.3 %shard_map.46 = f32[768,1024]{1,0:T(8,128)S(1)} custom-call(s32[2,2]{1,0:T(2,128)S(1)} %copy-done, f32[2,384,1024]{2,1,0:T(8,128)} %bitcast.6, f32[1,128]{1,0:T(1,128)S(1)} %bitcast.4, f32[1,8]{1,0:T(1,128)S(1)} %bitcast.5), custom_call_target="tpu_custom_call" | custom-call | flops 19327352832 | bytes 6291456 | tf_op jit(solution)/shard_map/pallas_call | solution.py:183
  150.3 2.0 %neg.14 = f32[768,1024]{1,0:T(8,128)} negate(f32[768,1024]{1,0:T(8,128)S(1)} %shard_map.46) | non-fusion elementwise | flops 786432 | bytes 6291456 | tf_op jit(solution)/shard_map/neg | solution.py:216
Async XLA Ops:
  0.0 0.7 copy-start
  0.7 0.7 copy-start.1
  1.3 0.7 copy-start.2
